TPU v7x, 32 devices: a whole 2x2x4 slice. The times are simulated.
32 devices in a mesh: grp: 1, node: 32 (over z, y, x, core), dev: 1.
Axes of the slice: x: 2, y: 2, z: 4, core: 2. Of those that a mesh axis runs over, the one named last changes fastest.
Arguments:
- states: bfloat16 [256, 7168], P(('grp', 'node', 'dev')), may hold values from -6 to 6
- norm_gain: float32 [7168], replicated, may hold values from 0.1 to 1.9
- w_gate: bfloat16 [32, 7168, 512], P('node', None, 'dev'), may hold values from -0.0625 to 0.0625
- w_up: bfloat16 [32, 7168, 512], P('node', None, 'dev'), may hold values from -0.0625 to 0.0625
- w_down: bfloat16 [32, 512, 7168], P('node', 'dev'), may hold values from -0.125 to 0.125
- expert_ids: int32 [256, 2], P(('grp', 'node', 'dev')), may hold values from 0 to 7, all different within a row; in each aligned block of 8 rows (0 to 7, 8 to 15, ...) at most 4 rows name the same one
- route_weights: float32 [256, 2], P(('grp', 'node', 'dev')), may hold values from 0.5 to 2
- live_rows: int32 [256], P(('grp', 'node', 'dev')), may hold values 0 or 1
Outputs:
- mixed: bfloat16 [256, 7168], P(('grp', 'node', 'dev'))
Inputs may be any that keep to these rules, and one draw needn't show every extreme that they name: `expert_ids`: each row names 2 different experts. Among the rows of one device (aligned blocks of 8 rows) no expert is named by more than 4 rows, and in every draw some expert is named by exactly 4 rows of some device.
All inputs are finite; a program needn't handle non-finite values. No bound on the sum of `live_rows` on one device may be relied on, other than what follows from the above.
Results may differ from a plain program's by a relative error of at most 0.0052.
Values may be sent and summed in bfloat16 or wider, within the bound.
A program may use at most 128 MiB of HBM per device.

v0:
```python
import functools

import jax
import jax.numpy as jnp
from jax import lax
from jax.experimental import pallas as pl
from jax.experimental.pallas import tpu as pltpu
from jax.sharding import PartitionSpec as P

SPREAD = 4
norm_eps = 1e-06
F32 = jnp.float32
BF16 = jnp.bfloat16


def flip(value, bit):
    return value + bit - 2 * bit * ((value // bit) % 2)


def xor(value, mask):
    bit = 1
    while bit <= mask:
        if mask & bit:
            value = flip(value, bit)
        bit *= 2
    return value


def kernel(E, M, DEVC, states, gain, w_gate, w_up, w_down, ids, route, live, out,
           wg, wu, wd, s0, g0, s1, X, acc, send_r, recv_r, fin, ret, s4, g4,
           w_sem, s0_sem, s1_sem, s2_sem, r_sem, f_sem, s4_sem):
    rows, width = states.shape
    cols = width // M
    S = s1.shape[1]
    cap = S // M
    bits = []
    b = 1
    while b < M:
        bits.append(b)
        b *= 2
    grp = lax.axis_index("grp")
    node = lax.axis_index("node")
    dev = lax.axis_index("dev")
    g = node // SPREAD
    m = (node % SPREAD) * DEVC + dev

    def device(group, member):
        return (grp, group * SPREAD + member // DEVC, member % DEVC)

    def remote(src, dst, sems, at, target):
        return pltpu.make_async_remote_copy(
            src_ref=src, dst_ref=dst, send_sem=sems.at[0, at], recv_sem=sems.at[1, at],
            device_id=target, device_id_type=pl.DeviceIdType.MESH)

    w_copies = {}
    for r in range(M):
        j = xor(m, r)
        span = pl.ds(pl.multiple_of(j * cols, cols), cols)
        w_copies[0, r] = pltpu.make_async_copy(w_gate.at[0, span, :], wg.at[j], w_sem.at[0, r])
        w_copies[1, r] = pltpu.make_async_copy(w_up.at[0, span, :], wu.at[j], w_sem.at[1, r])
        w_copies[2, r] = pltpu.make_async_copy(w_down.at[0, :, span], wd.at[j], w_sem.at[2, r])
    for r in range(M):
        w_copies[0, r].start()
        w_copies[1, r].start()
    for r in reversed(range(M)):
        w_copies[2, r].start()

    barrier = pltpu.get_barrier_semaphore()
    for r in range(1, M):
        pl.semaphore_signal(barrier, inc=1, device_id=device(g, xor(m, r)),
                            device_id_type=pl.DeviceIdType.MESH)
    for k in range(1, E):
        pl.semaphore_signal(barrier, inc=1, device_id=device((g + k) % E, m),
                            device_id_type=pl.DeviceIdType.MESH)

    x = states[...].astype(F32)
    mean_square = jnp.mean(x * x, axis=1, keepdims=True)
    normed = (x * lax.rsqrt(mean_square + norm_eps) * gain[...]).astype(BF16).astype(F32)
    lane = lax.broadcasted_iota(jnp.int32, (rows, E * S), 1)
    row = lax.broadcasted_iota(jnp.int32, (rows, E * S), 0)
    expert = lane // S
    hit_weight = jnp.zeros((rows, E * S), F32)
    hit = jnp.zeros((rows, E * S), jnp.int32)
    for k in range(ids.shape[1]):
        here = ids[:, k:k + 1] == expert
        hit = hit + here.astype(jnp.int32)
        hit_weight = hit_weight + jnp.where(here, route[:, k:k + 1], 0.0)
    rank = jnp.zeros((rows, E * S), jnp.int32)
    for r in range(rows - 1):
        rank = rank + jnp.where(row > r, hit[r:r + 1, :], 0)
    placed = jnp.where(rank + m * cap == lane % S, hit_weight, 0.0)
    for j in range(M):
        s0[j, :, :cols] = normed[:, j * cols:(j + 1) * cols]
        s0[j, :, cols:] = placed

    pl.semaphore_wait(barrier, M - 1 + E - 1)

    c0 = []
    for r in reversed(range(1, M)):
        p = xor(m, r)
        c = remote(s0.at[p], g0.at[m], s0_sem, r, device(g, p))
        c.start()
        c0.append(c)
    g0[m] = s0[m]
    for c in c0:
        c.wait()
    place = g0[:, :, cols:].reshape(M * rows, E * S)
    mine = g0[:, :, :cols].reshape(M * rows, cols).astype(BF16)
    onehot = jnp.where(place > 0, 1.0, 0.0).T.astype(BF16)
    packed = jnp.dot(onehot, mine, preferred_element_type=F32).astype(BF16)
    s1[...] = packed.reshape(E, S, cols)

    c1 = []
    for k in range(1, E):
        e = (g + k) % E
        c = remote(s1.at[e], X.at[m, g], s1_sem, k, device(e, m))
        c.start()
        c1.append(c)
    X[m, g] = s1[g]
    order = [(g + E - k) % E for k in range(E)]
    c2 = {}

    def forward(block, r, bit):
        j = xor(m, r)
        c = remote(X.at[j, block[1]], X.at[j, block[1]], s2_sem, (r + bit) * E + block[0],
                   device(g, flip(m, bit)))
        c.start()
        c2[r + bit, block[0]] = c

    for k in range(E):
        if k:
            c1[k - 1].wait()
        for bit in reversed(bits):
            forward((k, order[k]), 0, bit)
    for r in sorted(range(1, M), key=lambda v: bin(v).count("1")):
        low = r & -r
        if low > 1:
            for k in range(E):
                c2[r, k].wait_recv()
                for bit in reversed(bits):
                    if bit < low:
                        forward((k, order[k]), r, bit)

    hid = wg.shape[2]
    gate = jnp.zeros((E * S, hid), F32)
    up = jnp.zeros((E * S, hid), F32)
    for r in range(M):
        j = xor(m, r)
        w_copies[0, r].wait()
        w_copies[1, r].wait()
        if r & 1:
            for k in range(E):
                c2[r, k].wait_recv()
        xs = X[j].reshape(E * S, cols)
        gate = gate + jnp.dot(xs, wg[j], preferred_element_type=F32)
        up = up + jnp.dot(xs, wu[j], preferred_element_type=F32)
    hidden = (gate / (1.0 + jnp.exp(-gate)) * up).astype(BF16)

    back = [(g + k + 1) % E for k in range(E)]
    cr = {}
    cf = []
    for r in reversed(range(M)):
        j = xor(m, r)
        w_copies[2, r].wait()
        part = jnp.dot(hidden, wd[j], preferred_element_type=F32)
        low = r & -r
        if low == 1:
            send_r[r - 1] = part.astype(BF16).reshape(E, S, cols)
        else:
            acc[...] = part.reshape(E, S, cols)
        for k in range(E):
            e = back[k]
            if low != 1:
                total = acc[e]
                for bit in bits:
                    if r & bit:
                        break
                    cr[r + bit, k].wait_recv()
                    total = total + recv_r[r + bit - 1, e].astype(F32)
                if r:
                    send_r[r - 1, e] = total.astype(BF16)
                else:
                    fin[e] = total.astype(BF16)
            if r:
                c = remote(send_r.at[r - 1, e], recv_r.at[r - 1, e], r_sem, r * E + k,
                           device(g, flip(m, low)))
                c.start()
                cr[r, k] = c
            elif k < E - 1:
                c = remote(fin.at[e], ret.at[g], f_sem, k, device(e, m))
                c.start()
                cf.append(c)
    ret[g] = fin[g]
    for c in cf:
        c.wait()
    place = g0[:, :, cols:].reshape(M * rows, E * S)
    high = place.astype(BF16)
    rest = (place - high.astype(F32)).astype(BF16)
    got = ret[...].reshape(E * S, cols)
    branch = (jnp.dot(high, got, preferred_element_type=F32)
              + jnp.dot(rest, got, preferred_element_type=F32))
    s4[...] = branch.reshape(M, rows, cols)
    c4 = []
    for r in reversed(range(1, M)):
        p = xor(m, r)
        c = remote(s4.at[p], g4.at[m], s4_sem, r, device(g, p))
        c.start()
        c4.append(c)
    g4[m] = s4[m]
    for c in c4:
        c.wait()
    for j in range(M):
        span = slice(j * cols, (j + 1) * cols)
        out[:, span] = (states[:, span].astype(F32) + live[...] * g4[j]).astype(BF16)
    for c in list(c2.values()) + list(cr.values()):
        c.wait_send()


def body(states, norm_gain, w_gate, w_up, w_down, expert_ids, route_weights, live_rows):
    rows, width = states.shape
    nodes = lax.axis_size("node")
    devc = lax.axis_size("dev")
    E = nodes // SPREAD
    M = SPREAD * devc
    cap = min(rows, rows * expert_ids.shape[1] // E * 2)
    S = cap * M
    cols = width // M
    hid = w_gate.shape[2]
    vmem = pl.BlockSpec(memory_space=pltpu.VMEM)
    hbm = pl.BlockSpec(memory_space=pl.ANY)
    dma = pltpu.SemaphoreType.DMA
    return pl.pallas_call(
        functools.partial(kernel, E, M, devc),
        out_shape=jax.ShapeDtypeStruct((rows, width), BF16),
        in_specs=[vmem, vmem, hbm, hbm, hbm, vmem, vmem, vmem],
        out_specs=vmem,
        scratch_shapes=[
            pltpu.VMEM((M, cols, hid), BF16),
            pltpu.VMEM((M, cols, hid), BF16),
            pltpu.VMEM((M, hid, cols), BF16),
            pltpu.VMEM((M, rows, cols + E * S), F32),
            pltpu.VMEM((M, rows, cols + E * S), F32),
            pltpu.VMEM((E, S, cols), BF16),
            pltpu.VMEM((M, E, S, cols), BF16),
            pltpu.VMEM((E, S, cols), F32),
            pltpu.VMEM((M - 1, E, S, cols), BF16),
            pltpu.VMEM((M - 1, E, S, cols), BF16),
            pltpu.VMEM((E, S, cols), BF16),
            pltpu.VMEM((E, S, cols), BF16),
            pltpu.VMEM((M, rows, cols), F32),
            pltpu.VMEM((M, rows, cols), F32),
            dma((3, M)), dma((2, M)), dma((2, E)), dma((2, M * E)), dma((2, M * E)),
            dma((2, E)), dma((2, M)),
        ],
        compiler_params=pltpu.CompilerParams(
            collective_id=0, has_side_effects=True, vmem_limit_bytes=56 * 1024 * 1024),
    )(states, norm_gain.reshape(1, width), w_gate, w_up, w_down, expert_ids, route_weights,
      live_rows.reshape(rows, 1).astype(F32))


def solution(mesh):
    placed = (
        P(("grp", "node", "dev"), None),
        P(),
        P("node", None, "dev"),
        P("node", None, "dev"),
        P("node", "dev", None),
        P(("grp", "node", "dev"), None),
        P(("grp", "node", "dev"), None),
        P(("grp", "node", "dev")),
    )
    return jax.shard_map(
        body, mesh=mesh, in_specs=placed, out_specs=P(("grp", "node", "dev"), None), check_vma=False
    )
```

profile of v0, /device:TPU:0, one launch (start us, length us, event | category | flops | bytes accessed | tf_op | source)
XLA Modules:
  0.0 57.4 jit_solution(16679346186939520635)
XLA Ops:
  0.0 0.7 %convert_bitcast_fusion = f32[8,1]{0,1:T(1,128)S(1)} fusion(s32[8]{0:T(128)} %param.15), kind=kLoop, calls=%fused_computation | loop fusion | flops 8 | bytes 64 | tf_op jit(solution)/shard_map/convert_element_type | solution.py:258
  0.7 0.7 %copy.11.live = f32[8,1]{1,0:T(8,128)} copy(f32[8,1]{0,1:T(1,128)S(1)} %convert_bitcast_fusion) | data formatting | bytes 64 | tf_op jit(solution)/shard_map/convert_element_type | solution.py:258
  1.3 1.3 %copy.9.ids = s32[8,2]{1,0:T(8,128)} copy(s32[8,2]{0,1:T(2,128)} %param.13) | data formatting | bytes 128 | tf_op args[5]
  2.7 1.3 %copy.10.route = f32[8,2]{1,0:T(8,128)} copy(f32[8,2]{0,1:T(2,128)} %param.14) | data formatting | bytes 128 | tf_op args[6]
  4.0 51.8 %shard_map.82 = bf16[8,7168]{1,0:T(8,128)(2,1)} custom-call(bf16[8,7168]{1,0:T(8,128)(2,1)} %states.1, f32[1,7168]{1,0:T(1,128)} %bitcast.3, bf16[1,7168,512]{2,1,0:T(8,128)(2,1)} %w_gate.1, bf16[1,7168,512]{2,1,0:T(8,128)(2,1)} %w_up.1, bf16[1,512,7168]{2,1,0:T(8,128)(2,1)} %w_down.1, s32[8,2]{1,0:T(8,128)} %copy.9.ids, f32[8,2]{1,0:T(8,128)} %copy.10.route, ...), custom_call_target="tpu_custom_call" | custom-call | tf_op jit(solution)/shard_map/pallas_call | solution.py:232
  55.8 1.6 %copy.13 = bf16[8,7168]{1,0:T(8,128)(2,1)} copy(bf16[8,7168]{1,0:T(8,128)(2,1)} %shard_map.82) | data formatting | bytes 229376
where the time goes:
time: 58.4 us; the launch traced here: 57.4 us
  Pallas kernels  51.8 us (89%)
  local copies, waits for them, and re-layouts  4.91 us (8%)
  other arithmetic  0.66 us (1%)
    pallas_call x1, Pallas kernels, body(): pl.pallas_call(functools.partial(kernel, E, M, devc), out_shape=jax.Shape...  51.8 us
    unnamed x3, local copies, waits for them, and re-layouts  4.24 us

commit v1 on v0

--- a/solution.py
+++ b/solution.py
@@ -26,6 +26,23 @@
     return value
 
 
+def fold(value, half):
+    rows, cols = value.shape
+    second = value[:, half:]
+    if cols < 2 * half:
+        second = jnp.concatenate([second, jnp.zeros((rows, 2 * half - cols), F32)], axis=1)
+    return jnp.concatenate([value[:, :half], second], axis=0)
+
+
+def unfold(value, cols):
+    rows, half = value.shape[0] // 2, value.shape[1]
+    return jnp.concatenate([value[:rows], value[rows:, :cols - half]], axis=1)
+
+
+def far_first(E):
+    return list(range(E - 1, 0, -1))
+
+
 def kernel(E, M, DEVC, states, gain, w_gate, w_up, w_down, ids, route, live, out,
            wg, wu, wd, s0, g0, s1, X, acc, send_r, recv_r, fin, ret, s4, g4,
            w_sem, s0_sem, s1_sem, s2_sem, r_sem, f_sem, s4_sem):
@@ -33,6 +50,7 @@
     cols = width // M
     S = s1.shape[1]
     cap = S // M
+    half = s4.shape[2]
     bits = []
     b = 1
     while b < M:
@@ -70,7 +88,7 @@
         pl.semaphore_signal(barrier, inc=1, device_id=device(g, xor(m, r)),
                             device_id_type=pl.DeviceIdType.MESH)
     for k in range(1, E):
-        pl.semaphore_signal(barrier, inc=1, device_id=device((g + k) % E, m),
+        pl.semaphore_signal(barrier, inc=1, device_id=device(xor(g, k), m),
                             device_id_type=pl.DeviceIdType.MESH)
 
     x = states[...].astype(F32)
@@ -78,20 +96,28 @@
     normed = (x * lax.rsqrt(mean_square + norm_eps) * gain[...]).astype(BF16).astype(F32)
     lane = lax.broadcasted_iota(jnp.int32, (rows, E * S), 1)
     row = lax.broadcasted_iota(jnp.int32, (rows, E * S), 0)
-    expert = lane // S
+    expert = (lane // S).astype(F32)
+    diagonal = (lax.broadcasted_iota(jnp.int32, (rows, rows), 0)
+                == lax.broadcasted_iota(jnp.int32, (rows, rows), 1))
+
+    def column(line):
+        spread = jnp.broadcast_to(line.astype(F32), (rows, rows))
+        return jnp.sum(jnp.where(diagonal, spread, 0.0), axis=1, keepdims=True)
+
     hit_weight = jnp.zeros((rows, E * S), F32)
     hit = jnp.zeros((rows, E * S), jnp.int32)
-    for k in range(ids.shape[1]):
-        here = ids[:, k:k + 1] == expert
+    for k in range(ids.shape[0]):
+        here = column(ids[k:k + 1, :]) == expert
         hit = hit + here.astype(jnp.int32)
-        hit_weight = hit_weight + jnp.where(here, route[:, k:k + 1], 0.0)
+        hit_weight = hit_weight + jnp.where(here, column(route[k:k + 1, :]), 0.0)
     rank = jnp.zeros((rows, E * S), jnp.int32)
     for r in range(rows - 1):
         rank = rank + jnp.where(row > r, hit[r:r + 1, :], 0)
     placed = jnp.where(rank + m * cap == lane % S, hit_weight, 0.0)
+    high = placed.astype(BF16).astype(F32)
     for j in range(M):
-        s0[j, :, :cols] = normed[:, j * cols:(j + 1) * cols]
-        s0[j, :, cols:] = placed
+        s0[j, :, :half] = fold(normed[:, j * cols:(j + 1) * cols], half).astype(BF16)
+        s0[j, :, half:] = jnp.concatenate([high, placed - high], axis=0).astype(BF16)
 
     pl.semaphore_wait(barrier, M - 1 + E - 1)
 
@@ -104,20 +130,23 @@
     g0[m] = s0[m]
     for c in c0:
         c.wait()
-    place = g0[:, :, cols:].reshape(M * rows, E * S)
-    mine = g0[:, :, :cols].reshape(M * rows, cols).astype(BF16)
+    got = [g0[r].astype(F32) for r in range(M)]
+    high = jnp.concatenate([v[:rows, half:] for v in got], axis=0)
+    rest = jnp.concatenate([v[rows:, half:] for v in got], axis=0)
+    place = high + rest
+    mine = jnp.concatenate([unfold(v[:, :half], cols) for v in got], axis=0).astype(BF16)
     onehot = jnp.where(place > 0, 1.0, 0.0).T.astype(BF16)
     packed = jnp.dot(onehot, mine, preferred_element_type=F32).astype(BF16)
     s1[...] = packed.reshape(E, S, cols)
 
-    c1 = []
-    for k in range(1, E):
-        e = (g + k) % E
+    c1 = {}
+    for k in far_first(E):
+        e = xor(g, k)
         c = remote(s1.at[e], X.at[m, g], s1_sem, k, device(e, m))
         c.start()
-        c1.append(c)
+        c1[k] = c
     X[m, g] = s1[g]
-    order = [(g + E - k) % E for k in range(E)]
+    order = [xor(g, k) for k in range(E)]
     c2 = {}
 
     def forward(block, r, bit):
@@ -129,18 +158,9 @@
 
     for k in range(E):
         if k:
-            c1[k - 1].wait()
+            c1[k].wait_recv()
         for bit in reversed(bits):
             forward((k, order[k]), 0, bit)
-    for r in sorted(range(1, M), key=lambda v: bin(v).count("1")):
-        low = r & -r
-        if low > 1:
-            for k in range(E):
-                c2[r, k].wait_recv()
-                for bit in reversed(bits):
-                    if bit < low:
-                        forward((k, order[k]), r, bit)
-
     hid = wg.shape[2]
     gate = jnp.zeros((E * S, hid), F32)
     up = jnp.zeros((E * S, hid), F32)
@@ -148,15 +168,18 @@
         j = xor(m, r)
         w_copies[0, r].wait()
         w_copies[1, r].wait()
-        if r & 1:
-            for k in range(E):
-                c2[r, k].wait_recv()
+        for k in range(E if r else 0):
+            c2[r, k].wait_recv()
+            for bit in reversed(bits):
+                if bit < (r & -r):
+                    forward((k, order[k]), r, bit)
         xs = X[j].reshape(E * S, cols)
         gate = gate + jnp.dot(xs, wg[j], preferred_element_type=F32)
         up = up + jnp.dot(xs, wu[j], preferred_element_type=F32)
     hidden = (gate / (1.0 + jnp.exp(-gate)) * up).astype(BF16)
 
-    back = [(g + k + 1) % E for k in range(E)]
+    turns = far_first(E) + [0]
+    back = [xor(g, k) for k in turns]
     cr = {}
     cf = []
     for r in reversed(range(M)):
@@ -187,19 +210,19 @@
                 c.start()
                 cr[r, k] = c
             elif k < E - 1:
-                c = remote(fin.at[e], ret.at[g], f_sem, k, device(e, m))
+                c = remote(fin.at[e], ret.at[g], f_sem, turns[k], device(e, m))
                 c.start()
                 cf.append(c)
     ret[g] = fin[g]
     for c in cf:
         c.wait()
-    place = g0[:, :, cols:].reshape(M * rows, E * S)
-    high = place.astype(BF16)
-    rest = (place - high.astype(F32)).astype(BF16)
+    high = high.astype(BF16)
+    rest = rest.astype(BF16)
     got = ret[...].reshape(E * S, cols)
     branch = (jnp.dot(high, got, preferred_element_type=F32)
               + jnp.dot(rest, got, preferred_element_type=F32))
-    s4[...] = branch.reshape(M, rows, cols)
+    for j in range(M):
+        s4[j] = fold(branch[j * rows:(j + 1) * rows], half).astype(BF16)
     c4 = []
     for r in reversed(range(1, M)):
         p = xor(m, r)
@@ -209,10 +232,11 @@
     g4[m] = s4[m]
     for c in c4:
         c.wait()
+    alive = column(live[...])
     for j in range(M):
         span = slice(j * cols, (j + 1) * cols)
-        out[:, span] = (states[:, span].astype(F32) + live[...] * g4[j]).astype(BF16)
-    for c in list(c2.values()) + list(cr.values()):
+        out[:, span] = (states[:, span].astype(F32) + alive * unfold(g4[j].astype(F32), cols)).astype(BF16)
+    for c in list(c1.values()) + list(c2.values()) + list(cr.values()):
         c.wait_send()
 
 
@@ -225,6 +249,7 @@
     cap = min(rows, rows * expert_ids.shape[1] // E * 2)
     S = cap * M
     cols = width // M
+    half = -(-cols // 256) * 128
     hid = w_gate.shape[2]
     vmem = pl.BlockSpec(memory_space=pltpu.VMEM)
     hbm = pl.BlockSpec(memory_space=pl.ANY)
@@ -238,8 +263,8 @@
             pltpu.VMEM((M, cols, hid), BF16),
             pltpu.VMEM((M, cols, hid), BF16),
             pltpu.VMEM((M, hid, cols), BF16),
-            pltpu.VMEM((M, rows, cols + E * S), F32),
-            pltpu.VMEM((M, rows, cols + E * S), F32),
+            pltpu.VMEM((M, 2 * rows, half + E * S), BF16),
+            pltpu.VMEM((M, 2 * rows, half + E * S), BF16),
             pltpu.VMEM((E, S, cols), BF16),
             pltpu.VMEM((M, E, S, cols), BF16),
             pltpu.VMEM((E, S, cols), F32),
@@ -247,15 +272,15 @@
             pltpu.VMEM((M - 1, E, S, cols), BF16),
             pltpu.VMEM((E, S, cols), BF16),
             pltpu.VMEM((E, S, cols), BF16),
-            pltpu.VMEM((M, rows, cols), F32),
-            pltpu.VMEM((M, rows, cols), F32),
+            pltpu.VMEM((M, 2 * rows, half), BF16),
+            pltpu.VMEM((M, 2 * rows, half), BF16),
             dma((3, M)), dma((2, M)), dma((2, E)), dma((2, M * E)), dma((2, M * E)),
             dma((2, E)), dma((2, M)),
         ],
         compiler_params=pltpu.CompilerParams(
             collective_id=0, has_side_effects=True, vmem_limit_bytes=56 * 1024 * 1024),
-    )(states, norm_gain.reshape(1, width), w_gate, w_up, w_down, expert_ids, route_weights,
-      live_rows.reshape(rows, 1).astype(F32))
+    )(states, norm_gain.reshape(1, width), w_gate, w_up, w_down, expert_ids.T, route_weights.T,
+      live_rows.reshape(1, rows))
 
 
 def solution(mesh):

time: 58.4 us -> 52.9 us (0.906); the launches traced: 57.4 us -> 52.7 us
  local copies, waits for them, and re-layouts: 4.91 us -> 1.55 us
  Pallas kernels: 51.8 us -> 51.1 us
  other arithmetic: 0.66 us -> 0 us
    unnamed x3 -> x1, local copies, waits for them, and re-layouts: 4.24 us -> 1.55 us
    convert_element_type x1 -> x0, local copies, waits for them, and re-layouts: 0.67 us -> none  [body(): live_rows.reshape(rows, 1).astype(F32)]
    convert_element_type x1 -> x0, other arithmetic: 0.66 us -> none  [body(): live_rows.reshape(rows, 1).astype(F32)]
    pallas_call x1, Pallas kernels: 51.8 us -> 51.1 us  [body(): pl.pallas_call(functools.partial(kernel, E, M, devc), out_shape=jax.Shape...]
where the time goes in v1:
time: 52.9 us; the launch traced here: 52.7 us
  Pallas kernels  51.1 us (97%)
  local copies, waits for them, and re-layouts  1.55 us (3%)
    pallas_call x1, Pallas kernels, body(): pl.pallas_call(functools.partial(kernel, E, M, devc), out_shape=jax.Shape...  51.1 us
    unnamed x1, local copies, waits for them, and re-layouts  1.55 us

profile of v1, /device:TPU:0, one launch (start us, length us, event | category | flops | bytes accessed | tf_op | source)
XLA Modules:
  0.0 52.7 jit_solution(2361564913054519216)
XLA Ops:
  0.0 51.1 %shard_map.82 = bf16[8,7168]{1,0:T(8,128)(2,1)} custom-call(bf16[8,7168]{1,0:T(8,128)(2,1)} %states.1, f32[1,7168]{1,0:T(1,128)} %bitcast.4, bf16[1,7168,512]{2,1,0:T(8,128)(2,1)} %w_gate.1, bf16[1,7168,512]{2,1,0:T(8,128)(2,1)} %w_up.1, bf16[1,512,7168]{2,1,0:T(8,128)(2,1)} %w_down.1, s32[2,8]{1,0:T(2,128)} %bitcast.5, f32[2,8]{1,0:T(2,128)} %bitcast.6, ...), custom_call_target="tpu_custom_call" | custom-call | tf_op jit(solution)/shard_map/pallas_call | solution.py:257
  51.1 1.6 %copy.10 = bf16[8,7168]{1,0:T(8,128)(2,1)} copy(bf16[8,7168]{1,0:T(8,128)(2,1)} %shard_map.82) | data formatting | bytes 229376

commit v2 on v1

--- a/solution.py
+++ b/solution.py
@@ -8,6 +8,8 @@
 from jax.sharding import PartitionSpec as P
 
 SPREAD = 4
+W = 4
+V = 2
 norm_eps = 1e-06
 F32 = jnp.float32
 BF16 = jnp.bfloat16
@@ -140,10 +142,11 @@
     s1[...] = packed.reshape(E, S, cols)
 
     c1 = {}
-    for k in far_first(E):
+    for k in list(range(E // 2, E)) + list(range(1, E // 2)):
         e = xor(g, k)
         c = remote(s1.at[e], X.at[m, g], s1_sem, k, device(e, m))
-        c.start()
+        if k < E // 2 + V:
+            c.start()
         c1[k] = c
     X[m, g] = s1[g]
     order = [xor(g, k) for k in range(E)]
@@ -159,6 +162,9 @@
     for k in range(E):
         if k:
             c1[k].wait_recv()
+        if k >= E // 2 and k + V < E:
+            c1[k].wait_send()
+            c1[k + V].start()
         for bit in reversed(bits):
             forward((k, order[k]), 0, bit)
     hid = wg.shape[2]
@@ -199,6 +205,8 @@
                     if r & bit:
                         break
                     cr[r + bit, k].wait_recv()
+                    if r == 0 and bit == M // 2 and k + W < E:
+                        cr[bit, k + W].start()
                     total = total + recv_r[r + bit - 1, e].astype(F32)
                 if r:
                     send_r[r - 1, e] = total.astype(BF16)
@@ -207,7 +215,8 @@
             if r:
                 c = remote(send_r.at[r - 1, e], recv_r.at[r - 1, e], r_sem, r * E + k,
                            device(g, flip(m, low)))
-                c.start()
+                if r != M // 2 or k < W:
+                    c.start()
                 cr[r, k] = c
             elif k < E - 1:
                 c = remote(fin.at[e], ret.at[g], f_sem, turns[k], device(e, m))
@@ -236,7 +245,8 @@
     for j in range(M):
         span = slice(j * cols, (j + 1) * cols)
         out[:, span] = (states[:, span].astype(F32) + alive * unfold(g4[j].astype(F32), cols)).astype(BF16)
-    for c in list(c1.values()) + list(c2.values()) + list(cr.values()):
+    late = [c1[k] for k in c1 if not E // 2 <= k < E - V]
+    for c in late + list(c2.values()) + list(cr.values()):
         c.wait_send()
 
 

time: 52.9 us -> 51.2 us (0.968)
  Pallas kernels: 51.1 us -> 49.5 us
    pallas_call x1, Pallas kernels: 51.1 us -> 49.5 us  [body(): pl.pallas_call(functools.partial(kernel, E, M, devc), out_shape=jax.Shape...]
where the time goes in v2:
time: 51.2 us; the launch traced here: 51 us
  Pallas kernels  49.5 us (97%)
  local copies, waits for them, and re-layouts  1.55 us (3%)
    pallas_call x1, Pallas kernels, body(): pl.pallas_call(functools.partial(kernel, E, M, devc), out_shape=jax.Shape...  49.5 us
    unnamed x1, local copies, waits for them, and re-layouts  1.55 us

profile of v2, /device:TPU:0, one launch (start us, length us, event | category | flops | bytes accessed | tf_op | source)
XLA Modules:
  0.0 51.0 jit_solution(4577164203177817765)
XLA Ops:
  0.0 49.5 %shard_map.82 = bf16[8,7168]{1,0:T(8,128)(2,1)} custom-call(bf16[8,7168]{1,0:T(8,128)(2,1)} %states.1, f32[1,7168]{1,0:T(1,128)} %bitcast.4, bf16[1,7168,512]{2,1,0:T(8,128)(2,1)} %w_gate.1, bf16[1,7168,512]{2,1,0:T(8,128)(2,1)} %w_up.1, bf16[1,512,7168]{2,1,0:T(8,128)(2,1)} %w_down.1, s32[2,8]{1,0:T(2,128)} %bitcast.5, f32[2,8]{1,0:T(2,128)} %bitcast.6, ...), custom_call_target="tpu_custom_call" | custom-call | tf_op jit(solution)/shard_map/pallas_call | solution.py:267
  49.5 1.6 %copy.10 = bf16[8,7168]{1,0:T(8,128)(2,1)} copy(bf16[8,7168]{1,0:T(8,128)(2,1)} %shard_map.82) | data formatting | bytes 229376

commit v3 on v2

--- a/solution.py
+++ b/solution.py
@@ -204,7 +204,8 @@
                 for bit in bits:
                     if r & bit:
                         break
-                    cr[r + bit, k].wait_recv()
+                    if bit > 1 or k == 0:
+                        cr[r + bit, k].wait_recv()
                     if r == 0 and bit == M // 2 and k + W < E:
                         cr[bit, k + W].start()
                     total = total + recv_r[r + bit - 1, e].astype(F32)
@@ -212,7 +213,12 @@
                     send_r[r - 1, e] = total.astype(BF16)
                 else:
                     fin[e] = total.astype(BF16)
-            if r:
+            if low == 1:
+                if k == 0:
+                    c = remote(send_r.at[r - 1], recv_r.at[r - 1], r_sem, r * E, device(g, flip(m, 1)))
+                    c.start()
+                    cr[r, 0] = c
+            elif r:
                 c = remote(send_r.at[r - 1, e], recv_r.at[r - 1, e], r_sem, r * E + k,
                            device(g, flip(m, low)))
                 if r != M // 2 or k < W:

time: 51.2 us -> 51.7 us (level)
    pallas_call x1, Pallas kernels: 49.5 us -> 50 us  [body(): pl.pallas_call(functools.partial(kernel, E, M, devc), out_shape=jax.Shape...]
where the time goes in v3:
time: 51.7 us; the launch traced here: 51.6 us
  Pallas kernels  50 us (97%)
  local copies, waits for them, and re-layouts  1.55 us (3%)
    pallas_call x1, Pallas kernels, body(): pl.pallas_call(functools.partial(kernel, E, M, devc), out_shape=jax.Shape...  50 us
    unnamed x1, local copies, waits for them, and re-layouts  1.55 us

profile of v3, /device:TPU:0, one launch (start us, length us, event | category | flops | bytes accessed | tf_op | source)
XLA Modules:
  0.0 51.6 jit_solution(11378937656105877921)
XLA Ops:
  0.0 50.0 %shard_map.82 = bf16[8,7168]{1,0:T(8,128)(2,1)} custom-call(bf16[8,7168]{1,0:T(8,128)(2,1)} %states.1, f32[1,7168]{1,0:T(1,128)} %bitcast.4, bf16[1,7168,512]{2,1,0:T(8,128)(2,1)} %w_gate.1, bf16[1,7168,512]{2,1,0:T(8,128)(2,1)} %w_up.1, bf16[1,512,7168]{2,1,0:T(8,128)(2,1)} %w_down.1, s32[2,8]{1,0:T(2,128)} %bitcast.5, f32[2,8]{1,0:T(2,128)} %bitcast.6, ...), custom_call_target="tpu_custom_call" | custom-call | tf_op jit(solution)/shard_map/pallas_call | solution.py:273
  50.0 1.6 %copy.10 = bf16[8,7168]{1,0:T(8,128)(2,1)} copy(bf16[8,7168]{1,0:T(8,128)(2,1)} %shard_map.82) | data formatting | bytes 229376
